TPU v7x, 32 devices: a whole 2x2x4 slice. The times are simulated.
32 devices in a mesh: blk: 8 (over y, x, core), orb: 4 (over z).
Axes of the slice: x: 2, y: 2, z: 4, core: 2. Of those that a mesh axis runs over, the one named last changes fastest.
Arguments:
- green_tiles: bfloat16 [2, 192, 256, 256], P(None, 'blk'), may hold values from -6 to 6
- screen_tiles: bfloat16 [2, 96, 256, 256], P(None, 'blk', 'orb'), may hold values from -6 to 6
- coeffs: bfloat16 [12288, 2048], P('blk', 'orb'), may hold values from -0.099609375 to 0.099609375
- tile_count: int32 [8], P('blk'), may hold values from 1 to 24, 96 in all
- send_slot: int32 [8, 8, 3], P('blk'), may hold values from 0 to 11
- recv_index: int32 [8, 24], P('blk'), may hold values from 0 to 23, as said below
- row_block: int32 [8, 24], P('blk'), may hold values from 0 to 5
- col_block: int32 [8, 24], P('blk'), may hold values from 0 to 47
Outputs:
- sigma_orbital: float32 [2048, 2, 2048], P('blk', None, 'orb')
Inputs may be any that keep to these rules, and one draw needn't show every extreme that they name: `recv_index`: for each blk index and each round r < 3, the slots r * (8) to (r + 1) * 8 - 1 name every peer once, each as peer * 3 + r. `tile_count`: the counts of all blk indices sum to 96.
All inputs are finite; a program needn't handle non-finite values. No bound on the sum of `tile_count` on one device may be relied on, other than what follows from the above.
Results may differ from a plain program's by a relative error of at most 0.0041.
Values may be sent and summed in bfloat16 or wider, within the bound.
A program may use at most 128 MiB of HBM per device.

v0:
```python
import jax
import jax.numpy as jnp
from jax import lax
from jax.sharding import PartitionSpec as P


def shards(
    green_tiles, screen_tiles, coeffs, tile_count, send_slot, recv_index, row_block, col_block
):
    width = green_tiles.shape[2]
    slot_total = green_tiles.shape[1]
    owned_blocks = coeffs.shape[0] // width
    orbital_local = coeffs.shape[1]
    outgoing = send_slot.reshape(-1)
    screen_whole = lax.all_gather(screen_tiles, "orb", axis=2, tiled=True)
    packed = jnp.take(screen_whole, outgoing, axis=1)
    arrived = lax.all_to_all(packed, "blk", split_axis=1, concat_axis=1, tiled=True)
    panel = lax.all_gather(coeffs, "blk", axis=0, tiled=True)
    panel_blocks = panel.reshape(-1, width, orbital_local)
    own_rows = lax.all_gather(coeffs, "orb", axis=1, tiled=True)
    live = (jnp.arange(slot_total, dtype=jnp.int32) < tile_count[0]).astype(jnp.float32)
    targets = row_block[0]
    group = 8

    def accumulate(totals, start):
        green_part = lax.dynamic_slice_in_dim(green_tiles, start, group, 1)
        which = lax.dynamic_slice_in_dim(recv_index[0], start, group, 0)
        screen_part = jnp.take(arrived, which, axis=1)
        sigma = (-(green_part.astype(jnp.float32) * screen_part.astype(jnp.float32))).astype(
            jnp.bfloat16
        )
        columns = lax.dynamic_slice_in_dim(col_block[0], start, group, 0)
        blocks = jnp.take(panel_blocks, columns, axis=0)
        products = jnp.einsum("tsab,sbm->satm", sigma, blocks, preferred_element_type=jnp.float32)
        group_rows = lax.dynamic_slice_in_dim(targets, start, group, 0)
        group_live = lax.dynamic_slice_in_dim(live, start, group, 0)
        for member in range(group):
            target = group_rows[member]
            current = lax.dynamic_index_in_dim(totals, target, 0, keepdims=True)
            updated = current + group_live[member] * products[member][None]
            totals = lax.dynamic_update_slice_in_dim(totals, updated, target, 0)
        return (totals, None)

    starts = jnp.arange(0, slot_total, group, dtype=jnp.int32)
    empty = jnp.zeros((owned_blocks, width, 2, orbital_local), jnp.float32)
    totals, unused = lax.scan(accumulate, empty, starts)
    folded = totals.astype(jnp.bfloat16).reshape(owned_blocks * width, 2, orbital_local)
    return lax.psum_scatter(
        jnp.einsum("kn,ktm->ntm", own_rows, folded, preferred_element_type=jnp.float32),
        "blk",
        scatter_dimension=0,
        tiled=True,
    )


def solution(mesh):
    return jax.shard_map(
        shards,
        mesh=mesh,
        in_specs=(
            P(None, "blk", None, None),
            P(None, "blk", "orb", None),
            P("blk", "orb"),
            P("blk"),
            P("blk", None, None),
            P("blk", None),
            P("blk", None),
            P("blk", None),
        ),
        out_specs=P("blk", None, "orb"),
        check_vma=False,
    )
```

profile of v0, /device:TPU:0, one launch (start us, length us, event | category | flops | bytes accessed | tf_op | source)
XLA Modules:
  0.0 496.9 jit_solution(7030310610212735367)
XLA Ops:
  6.5 0.7 all-gather.6.cloned.1.call-update
  7.3 0.7 all-gather.4.cloned.1.call-update
  8.0 0.8 copy.15
  8.8 0.1 reshape.117
  9.0 66.2 %all-gather.6.cloned.1.call-done = bf16[2,12,256,256]{3,2,1,0:T(8,128)(2,1)} async-done(((bf16[2,12,64,256]{3,2,1,0:T(8,128)(2,1)}), bf16[2,12,256,256]{3,2,1,0:T(8,128)(2,1)}) %all-gather.6.cloned.1.call-update) | async-done | bytes 3145744 | tf_op jit(solution)/shard_map/all_gather | solution.py:15
  75.1 6.3 %gather_fusion.2 = bf16[24,2,256,256]{3,2,1,0:T(8,128)(2,1)} fusion(bf16[2,12,256,256]{3,2,1,0:T(8,128)(2,1)} %all-gather.6.cloned.1.call-done, s32[1024]{0:T(1024)S(1)} %pad_clamp_fusion.2), kind=kCustom, calls=%fused_computation.2 | custom fusion | bytes 12583008 | tf_op jit(solution)/shard_map/jit(_take)/gather | solution.py:16
  81.4 7.0 %select_bitcast_fusion = bf16[2,24,256,256]{3,2,0,1:T(8,128)(2,1)} fusion(bf16[24,2,256,256]{3,2,1,0:T(8,128)(2,1)} %gather_fusion.2, pred[24]{0:T(512)(128)(4,1)S(1)} %compare_and_fusion.2), kind=kLoop, calls=%fused_computation.55 | loop fusion | flops 3145728 | bytes 12582936 | tf_op jit(solution)/shard_map/jit(_take)/select_n | solution.py:16
  88.4 4.8 all-to-all-start
  93.3 0.7 all-gather.8.cloned.1.call-update
  94.7 108.7 %all-to-all-done = bf16[2,24,256,256]{3,2,0,1:T(8,128)(2,1)} async-done(((bf16[2,24,256,256]{3,2,0,1:T(8,128)(2,1)}), bf16[2,24,256,256]{3,2,0,1:T(8,128)(2,1)}, u32[]{:S(2)}, u32[]{:S(2)}) %all-to-all-start) | async-done | bytes 6291488 | tf_op jit(solution)/shard_map/all_to_all | solution.py:17
  203.4 6.1 %copy.18 = bf16[2,24,256,256]{3,2,1,0:T(8,128)(2,1)} copy(bf16[2,24,256,256]{3,2,0,1:T(8,128)(2,1)} %all-to-all-done) | data formatting | bytes 12582912 | tf_op jit(solution)/shard_map/while | solution.py:46
  209.5 3.2 broadcast_in_dim.33
  212.8 189.6 %while.10 = (s32[]{:T(128)}, f32[6,256,2,512]{1,3,2,0:T(8,128)}, s32[3]{0:T(128)S(1)}, s32[24]{0:T(128)S(1)}, f32[24]{0:T(128)S(1)}, /*index=5*/s32[1,24]{1,0:T(...) while((s32[]{:T(128)}, f32[6,256,2,512]{1,3,2,0:T(8,128)}, ...), condition=%wide.region_1.2_spmd, body=%wide.region_0.1_spmd.sunk | while | flops 1085278336 | bytes 48247880 | solution.py:46
  212.8 0.7 dynamic_slice.98
  215.5 0.1 fusion.55
  215.6 4.2 gather_fusion
  219.8 6.9 %gather_fusion.1 = bf16[8,256,512]{2,1,0:T(8,128)(2,1)} fusion(bf16[48,256,512]{2,1,0:T(8,128)(2,1)} %get-tuple-element.253, s32[1024]{0:T(1024)S(1)} %pad_clamp_fusion.6), kind=kCustom, calls=%fused_computation.clone.1 | custom fusion | bytes 4194336 | tf_op jit(solution)/shard_map/while/body/eval_jaxpr/jit(_take)/gather | solution.py:33
  226.8 7.5 %convolution_bitcast_fusion.2 = f32[8,256,2,512]{1,3,2,0:T(8,128)} fusion(bf16[8,2,256,256]{3,2,1,0:T(8,128)(2,1)S(1)} %gather_fusion, bf16[8,256,512]{2,1,0:T(8,128)(2,1)} %gather_fusion.1, pred[8]{0:T(512)(128)(4,1)S(1)} %get-tuple-element.202, pred[8]{0:T(512)(128)(4,1)S(1)} %get-tuple-element.203, ...), kind=kOutput, calls=%fused_computation.6.clone.1 | convolution fusion | flops 1081081856 | bytes 14680084 | tf_op jit(solution)/shard_map/while/body/eval_jaxpr/tsab,sbm->satm/dot_general | solution.py:34
  234.3 0.7 fusion.54
  237.0 0.1 dynamic_slice.100
  237.1 0.7 fusion.56
  237.7 3.3 fusion.57
  242.7 3.2 fusion.58
  247.6 3.3 fusion.59
  252.8 3.3 fusion.60
  258.0 3.3 fusion.61
  263.1 3.3 fusion.62
  268.0 3.3 fusion.63
  273.3 3.4 fusion.64
  276.6 0.7 dynamic_slice.98
  279.4 0.1 fusion.55
  279.4 3.5 gather_fusion
  282.9 6.7 %gather_fusion.1 = bf16[8,256,512]{2,1,0:T(8,128)(2,1)} fusion(bf16[48,256,512]{2,1,0:T(8,128)(2,1)} %get-tuple-element.253, s32[1024]{0:T(1024)S(1)} %pad_clamp_fusion.6), kind=kCustom, calls=%fused_computation.clone.1 | custom fusion | bytes 4194336 | tf_op jit(solution)/shard_map/while/body/eval_jaxpr/jit(_take)/gather | solution.py:33
  289.7 7.4 %convolution_bitcast_fusion.2 = f32[8,256,2,512]{1,3,2,0:T(8,128)} fusion(bf16[8,2,256,256]{3,2,1,0:T(8,128)(2,1)S(1)} %gather_fusion, bf16[8,256,512]{2,1,0:T(8,128)(2,1)} %gather_fusion.1, pred[8]{0:T(512)(128)(4,1)S(1)} %get-tuple-element.202, pred[8]{0:T(512)(128)(4,1)S(1)} %get-tuple-element.203, ...), kind=kOutput, calls=%fused_computation.6.clone.1 | convolution fusion | flops 1081081856 | bytes 14680084 | tf_op jit(solution)/shard_map/while/body/eval_jaxpr/tsab,sbm->satm/dot_general | solution.py:34
  297.2 0.7 fusion.54
  299.9 0.1 dynamic_slice.100
  300.0 0.7 fusion.56
  300.7 3.3 fusion.57
  305.7 3.2 fusion.58
  310.6 3.3 fusion.59
  315.7 3.3 fusion.60
  320.9 3.3 fusion.61
  326.0 3.3 fusion.62
  331.0 3.3 fusion.63
  336.2 3.3 fusion.64
  339.5 0.7 dynamic_slice.98
  342.4 3.5 gather_fusion
  345.8 6.6 %gather_fusion.1 = bf16[8,256,512]{2,1,0:T(8,128)(2,1)} fusion(bf16[48,256,512]{2,1,0:T(8,128)(2,1)} %get-tuple-element.253, s32[1024]{0:T(1024)S(1)} %pad_clamp_fusion.6), kind=kCustom, calls=%fused_computation.clone.1 | custom fusion | bytes 4194336 | tf_op jit(solution)/shard_map/while/body/eval_jaxpr/jit(_take)/gather | solution.py:33
  352.5 7.4 %convolution_bitcast_fusion.2 = f32[8,256,2,512]{1,3,2,0:T(8,128)} fusion(bf16[8,2,256,256]{3,2,1,0:T(8,128)(2,1)S(1)} %gather_fusion, bf16[8,256,512]{2,1,0:T(8,128)(2,1)} %gather_fusion.1, pred[8]{0:T(512)(128)(4,1)S(1)} %get-tuple-element.202, pred[8]{0:T(512)(128)(4,1)S(1)} %get-tuple-element.203, ...), kind=kOutput, calls=%fused_computation.6.clone.1 | convolution fusion | flops 1081081856 | bytes 14680084 | tf_op jit(solution)/shard_map/while/body/eval_jaxpr/tsab,sbm->satm/dot_general | solution.py:34
  360.0 0.7 fusion.54
  362.7 0.1 dynamic_slice.100
  362.8 0.7 fusion.56
  363.5 3.2 fusion.57
  368.4 3.2 fusion.58
  373.3 3.3 fusion.59
  378.5 3.3 fusion.60
  383.7 3.3 fusion.61
  388.9 3.3 fusion.62
  393.9 3.3 fusion.63
  399.0 3.3 fusion.64
  402.4 4.0 copy.19
  406.4 10.8 %fusion.32 = f32[2048,2,512]{0,2,1:T(8,128)} fusion(bf16[1536,2,512]{2,0,1:T(8,128)(2,1)S(1)} %bitcast.107, bf16[1536,2048]{1,0:T(8,128)(2,1)} %all-gather.8.cloned.1.call-done), kind=kOutput, calls=%fused_computation.56 | convolution fusion | flops 6442450944 | bytes 17825792 | tf_op jit(solution)/shard_map/kn,ktm->ntm/dot_general | solution.py:49
  417.2 70.9 %reduce-scatter.2.cloned.1.call-done = f32[256,2,512]{0,2,1:T(8,128)} async-done(((f32[2048,2,512]{0,2,1:T(8,128)}), f32[256,2,512]{0,2,1:T(8,128)}) %reduce-scatter.2.cloned.1.call-update) | async-done | bytes 1048592 | tf_op jit(solution)/shard_map/reduce_scatter | solution.py:48
  488.1 2.2 copy.21
  (32 shorter events, 0.9 us)
Async XLA Ops:
  6.5 68.6 %all-gather.6.cloned.1.call-start = ((), (), s32[]{:S(2)}) async-start(), calls=%async_computation.3 | async-start | bytes 3932160 | tf_op jit(solution)/shard_map/all_gather | solution.py:15
  7.3 202.3 %all-gather.4.cloned.1.call-start = ((), (), s32[]{:S(2)}) async-start(), calls=%async_computation.2 | async-start | bytes 14155776 | tf_op jit(solution)/shard_map/all_gather | solution.py:18
  88.4 115.0 %all-to-all-start = ((bf16[2,24,256,256]{3,2,0,1:T(8,128)(2,1)}), bf16[2,24,256,256]{3,2,0,1:T(8,128)(2,1)}, u32[]{:S(2)}, u32[]{:S(2)}) async-start(bf16[2,24,256,256]{3,2,0,1:T(8,128)(2,1)} %select_bitcast_fusion), calls=%async_computation | async-start | bytes 12582912 | tf_op jit(solution)/shard_map/all_to_all | solution.py:17
  93.2 313.2 %all-gather.8.cloned.1.call-start = ((), (), s32[]{:S(2)}) async-start(), calls=%async_computation.4 | async-start | bytes 7864320 | tf_op jit(solution)/shard_map/all_gather | solution.py:20
  93.9 394.2 %reduce-scatter.2.cloned.1.call-start = ((), (), s32[]{:S(2)}) async-start(), calls=%async_computation.5 | async-start | bytes 9437184 | tf_op jit(solution)/shard_map/reduce_scatter | solution.py:48
  209.5 3.3 copy-start
  209.5 3.3 copy-start.1
  209.5 3.3 copy-start.2
Sparse Core Ops, SparseCore 0:
  8.9 66.1 all-gather.5
  77.0 130.5 all-gather.3
  209.2 115.3 all-gather.7
  417.4 70.7 reduce-scatter.1
where the time goes:
time: 499 us; the launch traced here: 497 us
  waiting for transfers between devices  248 us (50%)
  other arithmetic  86.3 us (17%)
  local copies, waits for them, and re-layouts  60.6 us (12%)
  loops' own time  50.2 us (10%)
  matrix products  33.2 us (7%)
  between operations  13.8 us (3%)
    all_to_all x1, waiting for transfers between devices, shards(): lax.all_to_all(packed, 'blk', split_axis=1, concat_axis=1, tiled=True)  109 us
    dynamic_update_slice x24, other arithmetic, accumulate(): totals = lax.dynamic_update_slice_in_dim(totals, updated, target, 0)  78.8 us
    reduce_scatter x1, waiting for transfers between devices, shards(): lax.psum_scatter(jnp.einsum('kn,ktm->ntm', own_rows, folded, preferred_el...  70.9 us
    all_gather x1, waiting for transfers between devices, shards(): screen_whole = lax.all_gather(screen_tiles, 'orb', axis=2, tiled=True)  66.2 us
    another operation x1, loops' own time, shards(): totals, unused = lax.scan(accumulate, empty, starts)  50.2 us
    dot_general x3, matrix products, accumulate(): jnp.einsum('tsab,sbm->satm', sigma, blocks, preferred_element_type=jnp.fl...  22.3 us
    gather x3, local copies, waits for them, and re-layouts, accumulate(): blocks = jnp.take(panel_blocks, columns, axis=0)  20.2 us
    gather x3, local copies, waits for them, and re-layouts, accumulate(): screen_part = jnp.take(arrived, which, axis=1)  11.1 us
  transfers between devices with their start and end apart: 5, of which 3 were waited for; matrix products, arithmetic and copies ran while one was open for 34% of the time, Pallas kernels for 0%

commit v1 on v0

--- a/solution.py
+++ b/solution.py
@@ -12,7 +12,22 @@
     owned_blocks = coeffs.shape[0] // width
     orbital_local = coeffs.shape[1]
     outgoing = send_slot.reshape(-1)
-    screen_whole = lax.all_gather(screen_tiles, "orb", axis=2, tiled=True)
+    ways, here, step = (lax.axis_size("orb"), lax.axis_index("orb"), screen_tiles.shape[2])
+    shape = [n * ways if d == 2 else n for d, n in enumerate(screen_tiles.shape)]
+    screen_whole = lax.dynamic_update_slice_in_dim(
+        jnp.zeros(shape, screen_tiles.dtype), screen_tiles, here * step, axis=2
+    )
+    going_up = going_down = screen_tiles
+    for far in range(1, ways // 2 + 1):
+        going_up = lax.ppermute(going_up, "orb", [(d, (d + 1) % ways) for d in range(ways)])
+        screen_whole = lax.dynamic_update_slice_in_dim(
+            screen_whole, going_up, (here - far) % ways * step, axis=2
+        )
+        if 2 * far < ways:
+            going_down = lax.ppermute(going_down, "orb", [(d, (d - 1) % ways) for d in range(ways)])
+            screen_whole = lax.dynamic_update_slice_in_dim(
+                screen_whole, going_down, (here + far) % ways * step, axis=2
+            )
     packed = jnp.take(screen_whole, outgoing, axis=1)
     arrived = lax.all_to_all(packed, "blk", split_axis=1, concat_axis=1, tiled=True)
     panel = lax.all_gather(coeffs, "blk", axis=0, tiled=True)

time: 499 us -> 445 us (0.89)
  waiting for transfers between devices: 248 us -> 187 us
  starting transfers between devices: 4.94 us -> 10.1 us
    all_gather x1 -> x0, waiting for transfers between devices: 66.2 us -> none  [shards(): screen_whole = lax.all_gather(screen_tiles, 'orb', axis=2, tiled=True)]
    ppermute x0 -> x3, waiting for transfers between devices: none -> 46.4 us  [the longest x2 33.6 us: shards(): lax.ppermute(going_up, 'orb', [(d, (d + 1) % ways) for d in range(ways)])]
    all_to_all x1, waiting for transfers between devices: 109 us -> 70.1 us  [shards(): lax.all_to_all(packed, 'blk', split_axis=1, concat_axis=1, tiled=True)]
    ppermute x0 -> x3, starting transfers between devices: none -> 5.17 us  [the longest x2 3.08 us: shards(): lax.ppermute(going_up, 'orb', [(d, (d + 1) % ways) for d in range(ways)])]
  transfers between devices with their start and end apart: 5 -> 7, of which waited for: 3 -> 5; matrix products, arithmetic and copies ran while one was open for 34% -> 38% of each run, Pallas kernels for 0% -> 0%
where the time goes in v1:
time: 445 us; the launch traced here: 443 us
  waiting for transfers between devices  187 us (42%)
  other arithmetic  85.4 us (19%)
  local copies, waits for them, and re-layouts  63 us (14%)
  loops' own time  50.2 us (11%)
  matrix products  33.1 us (7%)
  between operations  13.8 us (3%)
  starting transfers between devices  10.1 us (2%)
    dynamic_update_slice x24, other arithmetic, accumulate(): totals = lax.dynamic_update_slice_in_dim(totals, updated, target, 0)  78.7 us
    all_to_all x1, waiting for transfers between devices, shards(): lax.all_to_all(packed, 'blk', split_axis=1, concat_axis=1, tiled=True)  70.1 us
    reduce_scatter x1, waiting for transfers between devices, shards(): lax.psum_scatter(jnp.einsum('kn,ktm->ntm', own_rows, folded, preferred_el...  69.3 us
    another operation x1, loops' own time, shards(): totals, unused = lax.scan(accumulate, empty, starts)  50.2 us
    ppermute x2, waiting for transfers between devices, shards(): lax.ppermute(going_up, 'orb', [(d, (d + 1) % ways) for d in range(ways)])  33.6 us
    dot_general x3, matrix products, accumulate(): jnp.einsum('tsab,sbm->satm', sigma, blocks, preferred_element_type=jnp.fl...  22.3 us
    gather x3, local copies, waits for them, and re-layouts, accumulate(): blocks = jnp.take(panel_blocks, columns, axis=0)  19.9 us
    ppermute x1, waiting for transfers between devices, shards(): lax.ppermute(going_down, 'orb', [(d, (d - 1) % ways) for d in range(ways)])  12.8 us
  transfers between devices with their start and end apart: 7, of which 5 were waited for; matrix products, arithmetic and copies ran while one was open for 38% of the time, Pallas kernels for 0%

profile of v1, /device:TPU:0, one launch (start us, length us, event | category | flops | bytes accessed | tf_op | source)
XLA Modules:
  0.0 442.9 jit_solution(3038393809071013155)
XLA Ops:
  6.5 0.7 all-gather.3.cloned.1.call-update
  7.3 3.1 collective-permute-start
  10.3 2.1 collective-permute-start.1
  12.4 0.8 copy.15
  13.3 17.8 %collective-permute-done = bf16[2,12,64,256]{3,2,1,0:T(8,128)(2,1)} collective-permute-done((bf16[2,12,64,256]{3,2,1,0:T(8,128)(2,1)}, bf16[2,12,64,256]{3,2,1,0:T(8,128)(2,1)}, u32[]{:S(2)}, u32[]{:S(2)}) %collective-permute-start) | collective-permute-done | bytes 786464 | tf_op jit(solution)/shard_map/ppermute | solution.py:22
  31.5 1.2 constant_dynamic-update-slice_fusion.3
  32.7 1.2 constant_dynamic-update-slice_fusion.2
  33.9 12.8 %collective-permute-done.1 = bf16[2,12,64,256]{3,2,1,0:T(8,128)(2,1)} collective-permute-done((bf16[2,12,64,256]{3,2,1,0:T(8,128)(2,1)}, bf16[2,12,64,256]{3,2,1,0:T(8,128)(2,1)}, u32[]{:S(2)}, u32[]{:S(2)}) %collective-permute-start.1) | collective-permute-done | bytes 786464 | tf_op jit(solution)/shard_map/ppermute | solution.py:27
  46.7 1.4 constant_dynamic-update-slice_fusion.1
  48.1 15.8 %collective-permute-done.2 = bf16[2,12,64,256]{3,2,1,0:T(8,128)(2,1)} collective-permute-done((bf16[2,12,64,256]{3,2,1,0:T(8,128)(2,1)}, bf16[2,12,64,256]{3,2,1,0:T(8,128)(2,1)}, u32[]{:S(2)}, u32[]{:S(2)}) %collective-permute-start.2) | collective-permute-done | bytes 786464 | tf_op jit(solution)/shard_map/ppermute | solution.py:22
  64.0 1.2 constant_dynamic-update-slice_fusion
  65.2 4.4 gather_fusion.2
  69.6 6.1 %select_bitcast_fusion = bf16[2,24,256,256]{3,2,0,1:T(8,128)(2,1)} fusion(bf16[24,2,256,256]{3,2,1,0:T(8,128)(2,1)} %gather_fusion.2, pred[24]{0:T(512)(128)(4,1)S(1)} %compare_and_fusion.2), kind=kLoop, calls=%fused_computation.55 | loop fusion | flops 3145728 | bytes 12582936 | tf_op jit(solution)/shard_map/jit(_take)/select_n | solution.py:31
  75.7 4.8 %all-to-all-start = ((bf16[2,24,256,256]{3,2,0,1:T(8,128)(2,1)}), bf16[2,24,256,256]{3,2,0,1:T(8,128)(2,1)}, u32[]{:S(2)}, u32[]{:S(2)}) async-start(bf16[2,24,256,256]{3,2,0,1:T(8,128)(2,1)} %select_bitcast_fusion), calls=%async_computation | async-start | bytes 12582912 | tf_op jit(solution)/shard_map/all_to_all | solution.py:32
  80.6 0.7 all-gather.5.cloned.1.call-update
  82.0 70.1 %all-to-all-done = bf16[2,24,256,256]{3,2,0,1:T(8,128)(2,1)} async-done(((bf16[2,24,256,256]{3,2,0,1:T(8,128)(2,1)}), bf16[2,24,256,256]{3,2,0,1:T(8,128)(2,1)}, u32[]{:S(2)}, u32[]{:S(2)}) %all-to-all-start) | async-done | bytes 6291488 | tf_op jit(solution)/shard_map/all_to_all | solution.py:32
  152.1 6.2 %copy.18 = bf16[2,24,256,256]{3,2,1,0:T(8,128)(2,1)} copy(bf16[2,24,256,256]{3,2,0,1:T(8,128)(2,1)} %all-to-all-done) | data formatting | bytes 12582912 | tf_op jit(solution)/shard_map/while | solution.py:61
  158.3 3.2 broadcast_in_dim.36
  161.5 188.4 %while.10 = (s32[]{:T(128)}, f32[6,256,2,512]{1,3,2,0:T(8,128)}, s32[3]{0:T(128)S(1)}, s32[24]{0:T(128)S(1)}, f32[24]{0:T(128)S(1)}, /*index=5*/s32[1,24]{1,0:T(...) while((s32[]{:T(128)}, f32[6,256,2,512]{1,3,2,0:T(8,128)}, ...), condition=%wide.region_1.2_spmd, body=%wide.region_0.1_spmd.sunk | while | flops 1085278336 | bytes 48247880 | solution.py:61
  161.5 0.7 dynamic_slice.98
  164.4 3.5 gather_fusion
  167.9 6.7 %gather_fusion.1 = bf16[8,256,512]{2,1,0:T(8,128)(2,1)} fusion(bf16[48,256,512]{2,1,0:T(8,128)(2,1)} %get-tuple-element.253, s32[1024]{0:T(1024)S(1)} %pad_clamp_fusion.6), kind=kCustom, calls=%fused_computation.clone.1 | custom fusion | bytes 4194336 | tf_op jit(solution)/shard_map/while/body/eval_jaxpr/jit(_take)/gather | solution.py:48
  174.6 7.4 %convolution_bitcast_fusion.2 = f32[8,256,2,512]{1,3,2,0:T(8,128)} fusion(bf16[8,2,256,256]{3,2,1,0:T(8,128)(2,1)S(1)} %gather_fusion, bf16[8,256,512]{2,1,0:T(8,128)(2,1)} %gather_fusion.1, pred[8]{0:T(512)(128)(4,1)S(1)} %get-tuple-element.202, pred[8]{0:T(512)(128)(4,1)S(1)} %get-tuple-element.203, ...), kind=kOutput, calls=%fused_computation.6.clone.1 | convolution fusion | flops 1081081856 | bytes 14680084 | tf_op jit(solution)/shard_map/while/body/eval_jaxpr/tsab,sbm->satm/dot_general | solution.py:49
  182.1 0.7 fusion.54
  184.9 0.7 fusion.56
  185.6 3.3 fusion.57
  190.5 3.2 fusion.58
  195.4 3.3 fusion.59
  200.6 3.3 fusion.60
  205.7 3.3 fusion.61
  210.9 3.3 fusion.62
  215.8 3.3 fusion.63
  221.0 3.3 fusion.64
  224.4 0.7 dynamic_slice.98
  227.2 3.5 gather_fusion
  230.7 6.6 %gather_fusion.1 = bf16[8,256,512]{2,1,0:T(8,128)(2,1)} fusion(bf16[48,256,512]{2,1,0:T(8,128)(2,1)} %get-tuple-element.253, s32[1024]{0:T(1024)S(1)} %pad_clamp_fusion.6), kind=kCustom, calls=%fused_computation.clone.1 | custom fusion | bytes 4194336 | tf_op jit(solution)/shard_map/while/body/eval_jaxpr/jit(_take)/gather | solution.py:48
  237.3 7.4 %convolution_bitcast_fusion.2 = f32[8,256,2,512]{1,3,2,0:T(8,128)} fusion(bf16[8,2,256,256]{3,2,1,0:T(8,128)(2,1)S(1)} %gather_fusion, bf16[8,256,512]{2,1,0:T(8,128)(2,1)} %gather_fusion.1, pred[8]{0:T(512)(128)(4,1)S(1)} %get-tuple-element.202, pred[8]{0:T(512)(128)(4,1)S(1)} %get-tuple-element.203, ...), kind=kOutput, calls=%fused_computation.6.clone.1 | convolution fusion | flops 1081081856 | bytes 14680084 | tf_op jit(solution)/shard_map/while/body/eval_jaxpr/tsab,sbm->satm/dot_general | solution.py:49
  244.8 0.7 fusion.54
  247.6 0.7 fusion.56
  248.3 3.3 fusion.57
  253.3 3.2 fusion.58
  258.2 3.3 fusion.59
  263.3 3.3 fusion.60
  268.5 3.3 fusion.61
  273.6 3.3 fusion.62
  278.6 3.3 fusion.63
  283.8 3.3 fusion.64
  290.0 3.5 gather_fusion
  293.5 6.6 %gather_fusion.1 = bf16[8,256,512]{2,1,0:T(8,128)(2,1)} fusion(bf16[48,256,512]{2,1,0:T(8,128)(2,1)} %get-tuple-element.253, s32[1024]{0:T(1024)S(1)} %pad_clamp_fusion.6), kind=kCustom, calls=%fused_computation.clone.1 | custom fusion | bytes 4194336 | tf_op jit(solution)/shard_map/while/body/eval_jaxpr/jit(_take)/gather | solution.py:48
  300.1 7.4 %convolution_bitcast_fusion.2 = f32[8,256,2,512]{1,3,2,0:T(8,128)} fusion(bf16[8,2,256,256]{3,2,1,0:T(8,128)(2,1)S(1)} %gather_fusion, bf16[8,256,512]{2,1,0:T(8,128)(2,1)} %gather_fusion.1, pred[8]{0:T(512)(128)(4,1)S(1)} %get-tuple-element.202, pred[8]{0:T(512)(128)(4,1)S(1)} %get-tuple-element.203, ...), kind=kOutput, calls=%fused_computation.6.clone.1 | convolution fusion | flops 1081081856 | bytes 14680084 | tf_op jit(solution)/shard_map/while/body/eval_jaxpr/tsab,sbm->satm/dot_general | solution.py:49
  307.6 0.7 fusion.54
  310.4 0.7 fusion.56
  311.1 3.2 fusion.57
  316.0 3.2 fusion.58
  320.9 3.3 fusion.59
  326.1 3.3 fusion.60
  331.3 3.3 fusion.61
  336.5 3.3 fusion.62
  341.5 3.3 fusion.63
  346.6 3.3 fusion.64
  350.0 4.0 copy.19
  354.0 10.8 %fusion.32 = f32[2048,2,512]{0,2,1:T(8,128)} fusion(bf16[1536,2,512]{2,0,1:T(8,128)(2,1)S(1)} %bitcast.107, bf16[1536,2048]{1,0:T(8,128)(2,1)} %all-gather.5.cloned.1.call-done), kind=kOutput, calls=%fused_computation.56 | convolution fusion | flops 6442450944 | bytes 17825792 | tf_op jit(solution)/shard_map/kn,ktm->ntm/dot_general | solution.py:64
  364.8 69.3 %reduce-scatter.2.cloned.1.call-done = f32[256,2,512]{0,2,1:T(8,128)} async-done(((f32[2048,2,512]{0,2,1:T(8,128)}), f32[256,2,512]{0,2,1:T(8,128)}) %reduce-scatter.2.cloned.1.call-update) | async-done | bytes 1048592 | tf_op jit(solution)/shard_map/reduce_scatter | solution.py:63
  434.1 2.2 copy.21
  (40 shorter events, 2.3 us)
Async XLA Ops:
  6.5 151.8 %all-gather.3.cloned.1.call-start = ((), (), s32[]{:S(2)}) async-start(), calls=%async_computation.2 | async-start | bytes 14155776 | tf_op jit(solution)/shard_map/all_gather | solution.py:33
  7.3 23.8 %collective-permute-start = (bf16[2,12,64,256]{3,2,1,0:T(8,128)(2,1)}, bf16[2,12,64,256]{3,2,1,0:T(8,128)(2,1)}, u32[]{:S(2)}, u32[]{:S(2)}) collective-permute-start(bf16[2,12,64,256]{3,2,1,0:T(8,128)(2,1)} %param.11), channel_id=1, source_target_pairs={{0,1},{1,2},{2,3},{3,0},{4,5},{5,6},{6,7},{7,4},{8,9},{9,10},{10,1... | collective-permute-start | bytes 2359304 | tf_op jit(solution)/shard_map/ppermute | solution.py:22
  10.3 36.4 %collective-permute-start.1 = (bf16[2,12,64,256]{3,2,1,0:T(8,128)(2,1)}, bf16[2,12,64,256]{3,2,1,0:T(8,128)(2,1)}, u32[]{:S(2)}, u32[]{:S(2)}) collective-permute-start(bf16[2,12,64,256]{3,2,1,0:T(8,128)(2,1)} %param.11), channel_id=1, source_target_pairs={{0,3},{1,0},{2,1},{3,2},{4,7},{5,4},{6,5},{7,6},{8,11},{9,8},{10,9... | collective-permute-start | bytes 2359304 | tf_op jit(solution)/shard_map/ppermute | solution.py:27
  31.1 32.9 %collective-permute-start.2 = (bf16[2,12,64,256]{3,2,1,0:T(8,128)(2,1)}, bf16[2,12,64,256]{3,2,1,0:T(8,128)(2,1)}, u32[]{:S(2)}, u32[]{:S(2)}) collective-permute-start(bf16[2,12,64,256]{3,2,1,0:T(8,128)(2,1)} %collective-permute-done), channel_id=1, source_target_pairs={{0,1},{1,2},{2,3},{3,0},{4,5},{5,6},{6,7},{7,4},{8,9},{9,10},{10,1... | collective-permute-start | bytes 2359304 | tf_op jit(solution)/shard_map/ppermute | solution.py:22
  75.7 76.4 %all-to-all-start = ((bf16[2,24,256,256]{3,2,0,1:T(8,128)(2,1)}), bf16[2,24,256,256]{3,2,0,1:T(8,128)(2,1)}, u32[]{:S(2)}, u32[]{:S(2)}) async-start(bf16[2,24,256,256]{3,2,0,1:T(8,128)(2,1)} %select_bitcast_fusion), calls=%async_computation | async-start | bytes 12582912 | tf_op jit(solution)/shard_map/all_to_all | solution.py:32
  80.5 273.5 %all-gather.5.cloned.1.call-start = ((), (), s32[]{:S(2)}) async-start(), calls=%async_computation.3 | async-start | bytes 7864320 | tf_op jit(solution)/shard_map/all_gather | solution.py:35
  81.3 352.9 %reduce-scatter.2.cloned.1.call-start = ((), (), s32[]{:S(2)}) async-start(), calls=%async_computation.4 | async-start | bytes 9437184 | tf_op jit(solution)/shard_map/reduce_scatter | solution.py:63
  158.3 3.3 copy-start
  158.3 3.3 copy-start.1
  158.3 3.3 copy-start.2
Sparse Core Ops, SparseCore 0:
  9.2 74.8 all-gather.2
  85.7 115.3 all-gather.4
  365.0 69.1 reduce-scatter.1
